TPU v7x, 128 devices: a whole 4x4x4 slice. The times are simulated.
128 devices in a mesh: dp: 8 (over y, z_hi), ctx: 16 (over x, z_lo, core).
Axes of the slice: x: 4, y: 4, z: 4 (z_hi: 2, z_lo: 2; z = z_hi * 2 + z_lo), core: 2. Of those that a mesh axis runs over, the one named last changes fastest.
Arguments:
- inputs: bfloat16 [8, 2048, 4096], P('dp', 'ctx'), may hold values from -8 to 8
- queries: bfloat16 [8, 2048, 8192], P('dp', 'ctx'), may hold values from -256 to 256
- grad_output: bfloat16 [8, 2048, 8192], P('dp', 'ctx'), may hold values from -6 to 6
- kv_weight: bfloat16 [4096, 1024], P(('dp', 'ctx')), may hold values from -1 to 1
Outputs:
- attn_out: bfloat16 [8, 2048, 8192], P('dp', 'ctx')
- grad_query: bfloat16 [8, 2048, 8192], P('dp', 'ctx')
- grad_inputs: bfloat16 [8, 2048, 4096], P('dp', 'ctx')
- grad_weight: float32 [4096, 1024], P(('dp', 'ctx'))
All inputs are finite; a program needn't handle non-finite values.
Results may differ from a plain program's by a relative error of at most 0.035.
Values may be sent and summed in bfloat16 or wider, within the bound.
A program may use at most 128 MiB of HBM per device.

v0:
```python
import jax
import jax.numpy as jnp
from jax import lax
from jax.sharding import PartitionSpec as P

DH = 128
ROPE_BASE = 500000.0


def shifted(block, axis, distance):
    devices = range(lax.axis_size(axis))
    route = [(i - distance, i) for i in devices if i - distance in devices]
    return lax.ppermute(block, axis, route)


def shifted_2(value, axis, steps):
    count = lax.axis_size(axis)
    pairs = [(source, (source + steps) % count) for source in range(count)]
    return lax.ppermute(value, axis, pairs)


def rope_tables(positions, head_dim):
    half_dim = head_dim // 2
    frequency = ROPE_BASE ** (-2.0 * jnp.arange(half_dim, dtype=jnp.float32) / head_dim)
    angles = positions.astype(jnp.float32)[:, None] * frequency[None, :]
    return (jnp.cos(angles)[:, None, :], jnp.sin(angles)[:, None, :])


def rotary(values, positions):
    half_dim = values.shape[-1] // 2
    cosine, sine_table = rope_tables(positions, values.shape[-1])
    first_half = values[..., :half_dim]
    second = values[..., half_dim:]
    return jnp.concatenate(
        [first_half * cosine - second * sine_table, second * cosine + first_half * sine_table],
        axis=-1,
    )


def rotary_back(gradient, positions):
    half_dim = gradient.shape[-1] // 2
    cosine, sine_table = rope_tables(positions, gradient.shape[-1])
    first_half = gradient[..., :half_dim]
    second = gradient[..., half_dim:]
    return jnp.concatenate(
        [first_half * cosine + second * sine_table, second * cosine - first_half * sine_table],
        axis=-1,
    )


def on_device(inputs, queries, grad_output, kv_weight):
    token_count = inputs.shape[1]
    kv_width = kv_weight.shape[1]
    kv_half = kv_width // 2
    head_dim = DH
    kv_heads = kv_half // head_dim
    q_heads = queries.shape[2] // head_dim
    group_size = q_heads // kv_heads
    row_count = group_size * token_count
    ctx_size = lax.axis_size("ctx")
    ctx_index = lax.axis_index("ctx")
    score_scale = head_dim ** (-0.5)
    tokens = inputs[0]
    weight_all = lax.all_gather(kv_weight, ("dp", "ctx"), axis=0, tiled=True)
    projected = jnp.dot(tokens, weight_all, preferred_element_type=jnp.float32)
    positions = ctx_index * token_count + jnp.arange(token_count, dtype=jnp.int32)
    key_rows = rotary(
        projected[:, :kv_half].reshape(token_count, kv_heads, head_dim), positions
    ).astype(jnp.bfloat16)
    value_rows = projected[:, kv_half:].astype(jnp.bfloat16)
    own_block = jnp.concatenate([key_rows.reshape(token_count, kv_half), value_rows], axis=1)

    def head_rows(matrix):
        return (
            matrix.reshape(token_count, kv_heads, group_size, head_dim)
            .transpose(1, 2, 0, 3)
            .reshape(kv_heads, row_count, head_dim)
        )

    def token_rows(rows_by_head):
        return (
            rows_by_head.reshape(kv_heads, group_size, token_count, head_dim)
            .transpose(2, 0, 1, 3)
            .reshape(token_count, q_heads * head_dim)
        )

    query_rows = head_rows(queries[0])
    grad_rows = head_rows(grad_output[0])
    query_pos = jnp.arange(row_count, dtype=jnp.int32) % token_count
    key_pos = jnp.arange(token_count, dtype=jnp.int32)

    def split_block(kv_block):
        key_part = kv_block[:, :kv_half].reshape(token_count, kv_heads, head_dim)
        value_part = kv_block[:, kv_half:].reshape(token_count, kv_heads, head_dim)
        return (key_part, value_part)

    def block_scores(key_part, block_id):
        scores = (
            jnp.einsum("hrd,khd->hrk", query_rows, key_part, preferred_element_type=jnp.float32)
            * score_scale
        )
        allowed = (block_id < ctx_index) | (query_pos[:, None] >= key_pos[None, :])
        return (scores, allowed)

    def forward_update(state_now, kv_block, block_id):
        row_top, row_total, row_accum = state_now
        key_part, value_part = split_block(kv_block)
        scores, allowed = block_scores(key_part, block_id)
        scores = jnp.where(allowed[None], scores, -jnp.inf)
        new_top = jnp.maximum(row_top, jnp.max(scores, axis=-1, keepdims=True))
        weights = jnp.exp(scores - new_top)
        factor = jnp.exp(row_top - new_top)
        row_total = row_total * factor + jnp.sum(weights, axis=-1, keepdims=True)
        row_accum = row_accum * factor + jnp.einsum(
            "hrk,khd->hrd",
            weights.astype(jnp.bfloat16),
            value_part,
            preferred_element_type=jnp.float32,
        )
        return (new_top, row_total, row_accum)

    start_state = (
        jnp.full((kv_heads, row_count, 1), -jnp.inf, jnp.float32),
        jnp.zeros((kv_heads, row_count, 1), jnp.float32),
        jnp.zeros((kv_heads, row_count, head_dim), jnp.float32),
    )
    state_now = forward_update(start_state, own_block, ctx_index)
    kv_store = jnp.zeros((ctx_size, token_count, kv_width), jnp.bfloat16)
    kv_store = lax.dynamic_update_slice_in_dim(kv_store, own_block[None], ctx_index, 0)

    def forward_step(offset, loop_state):
        kv_block, stored_now, state_here = loop_state
        kv_block = shifted(kv_block, "ctx", 1)
        source = ctx_index - offset

        def take_block(operands):
            stored, current = operands
            stored = lax.dynamic_update_slice_in_dim(stored, kv_block[None], source, 0)
            return (stored, forward_update(current, kv_block, source))

        def keep_state(operands):
            return operands

        stored_now, state_here = lax.cond(
            offset <= ctx_index, take_block, keep_state, (stored_now, state_here)
        )
        return (kv_block, stored_now, state_here)

    last_block, kv_store, state_now = lax.fori_loop(
        1, ctx_size, forward_step, (own_block, kv_store, state_now)
    )
    row_top, row_total, row_accum = state_now
    attn_rows = (row_accum / row_total).astype(jnp.bfloat16)
    log_total = row_top + jnp.log(row_total)
    row_delta = jnp.sum(
        grad_rows.astype(jnp.float32) * attn_rows.astype(jnp.float32), axis=-1, keepdims=True
    )
    attn_out = token_rows(attn_rows)[None]

    def backward_terms(kv_block, block_id):
        key_part, value_part = split_block(kv_block)
        scores, allowed = block_scores(key_part, block_id)
        probs_now = jnp.where(allowed[None], jnp.exp(scores - log_total), 0.0)
        dprobs = jnp.einsum(
            "hrd,khd->hrk", grad_rows, value_part, preferred_element_type=jnp.float32
        )
        dscores = (probs_now * (dprobs - row_delta)).astype(jnp.bfloat16)
        grad_keys = (
            jnp.einsum("hrk,hrd->khd", dscores, query_rows, preferred_element_type=jnp.float32)
            * score_scale
        )
        grad_values = jnp.einsum(
            "hrk,hrd->khd",
            probs_now.astype(jnp.bfloat16),
            grad_rows,
            preferred_element_type=jnp.float32,
        )
        query_part = jnp.einsum(
            "hrk,khd->hrd", dscores, key_part, preferred_element_type=jnp.float32
        )
        block_grads = jnp.concatenate(
            [grad_keys.reshape(token_count, kv_half), grad_values.reshape(token_count, kv_half)],
            axis=1,
        )
        return (block_grads, query_part)

    def add_block(operands, block_id):
        grad_block, grad_query_sum = operands
        kv_block = lax.dynamic_slice_in_dim(kv_store, block_id, 1, 0)[0]
        block_grads, query_part = backward_terms(kv_block, block_id)
        return (grad_block + block_grads, grad_query_sum + query_part)

    def skip_block(operand_pair):
        return operand_pair

    zero_grads = jnp.zeros((token_count, kv_width), jnp.float32)
    zero_query = jnp.zeros((kv_heads, row_count, head_dim), jnp.float32)

    def backward_step(offset, operands):
        source = ctx_index - offset

        def include(operand_pair):
            return add_block(operand_pair, source)

        grad_block, grad_query_sum = lax.cond(offset <= ctx_index, include, skip_block, operands)
        grad_block = shifted_2(grad_block.astype(jnp.bfloat16), "ctx", 1).astype(grad_block.dtype)
        return (grad_block, grad_query_sum)

    grad_block, grad_query_sum = lax.fori_loop(0, ctx_size, backward_step, (zero_grads, zero_query))
    grad_query = token_rows(grad_query_sum * score_scale).astype(jnp.bfloat16)[None]
    grad_key_rows = rotary_back(
        grad_block[:, :kv_half].reshape(token_count, kv_heads, head_dim), positions
    ).reshape(token_count, kv_half)
    grad_projected = jnp.concatenate([grad_key_rows, grad_block[:, kv_half:]], axis=1).astype(
        jnp.bfloat16
    )
    grad_inputs = lax.dot_general(
        grad_projected, weight_all, (((1,), (1,)), ((), ())), preferred_element_type=jnp.float32
    ).astype(jnp.bfloat16)[None]
    grad_weight = lax.psum_scatter(
        lax.dot_general(
            tokens, grad_projected, (((0,), (0,)), ((), ())), preferred_element_type=jnp.float32
        ),
        ("dp", "ctx"),
        scatter_dimension=0,
        tiled=True,
    )
    return (attn_out, grad_query, grad_inputs, grad_weight)


def solution(mesh):
    in_specs = (
        P("dp", "ctx", None),
        P("dp", "ctx", None),
        P("dp", "ctx", None),
        P(("dp", "ctx"), None),
    )
    out_specs = (
        P("dp", "ctx", None),
        P("dp", "ctx", None),
        P("dp", "ctx", None),
        P(("dp", "ctx"), None),
    )
    return jax.shard_map(
        on_device, mesh=mesh, in_specs=in_specs, out_specs=out_specs, check_vma=False
    )
```

profile of v0, /device:TPU:0, one launch (start us, length us, event | category | flops | bytes accessed | tf_op | source)
XLA Modules:
  0.0 1567.8 jit_solution(14216864717612839760)
XLA Ops:
  8.0 2.2 copy.106
  10.2 3.8 copy.71
  14.0 2.8 reshape.234
  16.8 2.5 copy.76
  19.3 3.5 copy.108
  22.9 5.1 copy.79
  28.0 4.2 reshape.237
  33.4 182.2 %all-gather.2.cloned.1.call-done = bf16[4096,1024]{1,0:T(8,128)(2,1)} async-done(((bf16[32,1024]{1,0:T(8,128)(2,1)}), bf16[4096,1024]{1,0:T(8,128)(2,1)}) %all-gather.2.cloned.1.call-update) | async-done | bytes 8388624 | tf_op jit(solution)/shard_map/all_gather | solution.py:64
  215.6 4.6 fusion.28
  228.6 2.2 fusion.42
  231.5 3.3 convolution_add_fusion.1
  235.7 2.0 copy-done.6
  237.7 180.0 %while.38 = (s32[]{:T(128)}, bf16[128,1024]{0,1:T(8,128)(2,1)}, bf16[16,128,1024]{1,2,0:T(8,128)(2,1)}, f32[4,2048,1]{1,0,2:T(4,128)S(1)}, f32[4,2048,1]{1,0,2:T...) while((s32[]{:T(128)}, bf16[128,1024]{0,1:T(8,128)(2,1)}, ...), condition=%wide.region_7.8_spmd.clone, body=%wide.region_2.7_spmd.clone.sunk | while | flops 551063552 | bytes 61154760 | solution.py:149
  241.1 15.3 collective-permute-start
  258.4 6.5 collective-permute-start
  267.0 16.2 %collective-permute-start = (bf16[128,1024]{0,1:T(8,128)(2,1)}, bf16[128,1024]{0,1:T(8,128)(2,1)S(1)}, u32[]{:S(2)}, u32[]{:S(2)}) collective-permute-start(bf16[128,1024]{0,1:T(8,128)(2,1)} %get-tuple-element.838), channel_id=1, source_target_pairs={{0,1},{1,2},{2,3},{3,4},{4,5},{5,6},{6,7},{7,8},{8,9},{9,10},{10,1... | collective-permute-start | bytes 786440 | tf_op jit(solution)/shard_map/while/body/eval_jaxpr/ppermute | solution.py:13
  285.3 6.5 collective-permute-start
  293.9 12.5 collective-permute-start
  308.4 7.5 collective-permute-start
  318.0 17.1 %collective-permute-start = (bf16[128,1024]{0,1:T(8,128)(2,1)}, bf16[128,1024]{0,1:T(8,128)(2,1)S(1)}, u32[]{:S(2)}, u32[]{:S(2)}) collective-permute-start(bf16[128,1024]{0,1:T(8,128)(2,1)} %get-tuple-element.838), channel_id=1, source_target_pairs={{0,1},{1,2},{2,3},{3,4},{4,5},{5,6},{6,7},{7,8},{8,9},{9,10},{10,1... | collective-permute-start | bytes 786440 | tf_op jit(solution)/shard_map/while/body/eval_jaxpr/ppermute | solution.py:13
  337.1 7.4 collective-permute-start
  346.6 7.4 collective-permute-start
  356.1 7.4 collective-permute-start
  365.6 13.7 collective-permute-start
  381.3 7.4 collective-permute-start
  390.8 15.3 collective-permute-start
  408.2 7.4 collective-permute-start
  417.7 5.4 copy.77
  423.1 5.0 multiply_reduce_fusion
  428.1 2.2 broadcast.182
  430.3 439.3 %while.39 = (s32[]{:T(128)}, f32[128,1024]{0,1:T(8,128)}, f32[4,2048,128]{2,1,0:T(8,128)}, s32[]{:T(128)}, bf16[16,128,1024]{1,2,0:T(8,128)(2,1)}, /*index=5*/bf...) while((s32[]{:T(128)}, f32[128,1024]{0,1:T(8,128)}, ...), condition=%wide.region_12.13_spmd.clone, body=%wide.region_9.12_spmd.clone.sunk | while | flops 1351823360 | bytes 85468640 | solution.py:209
  431.1 11.4 conditional.7
  436.2 2.2 maximum_add_fusion
  438.4 2.2 convolution_add_fusion
  440.6 1.9 copy-done.5
  443.6 15.2 collective-permute-start.1
  458.9 85.0 %collective-permute-done.1 = bf16[128,1024]{0,1:T(8,128)(2,1)} collective-permute-done((bf16[128,1024]{0,1:T(8,128)(2,1)S(1)}, bf16[128,1024]{0,1:T(8,128)(2,1)}, u32[]{:S(2)}, u32[]{:S(2)}) %collective-permute-start.1) | collective-permute-done | bytes 262176 | tf_op jit(solution)/shard_map/while/body/eval_jaxpr/ppermute | solution.py:19
  545.7 1.9 broadcast_select_fusion.2
  548.7 14.7 collective-permute-done.1
  565.3 1.9 broadcast_select_fusion.2
  568.3 14.7 collective-permute-done.1
  587.9 14.7 collective-permute-done.1
  607.5 16.2 %collective-permute-done.1 = bf16[128,1024]{0,1:T(8,128)(2,1)} collective-permute-done((bf16[128,1024]{0,1:T(8,128)(2,1)S(1)}, bf16[128,1024]{0,1:T(8,128)(2,1)}, u32[]{:S(2)}, u32[]{:S(2)}) %collective-permute-start.1) | collective-permute-done | bytes 262176 | tf_op jit(solution)/shard_map/while/body/eval_jaxpr/ppermute | solution.py:19
  628.6 17.3 %collective-permute-done.1 = bf16[128,1024]{0,1:T(8,128)(2,1)} collective-permute-done((bf16[128,1024]{0,1:T(8,128)(2,1)S(1)}, bf16[128,1024]{0,1:T(8,128)(2,1)}, u32[]{:S(2)}, u32[]{:S(2)}) %collective-permute-start.1) | collective-permute-done | bytes 262176 | tf_op jit(solution)/shard_map/while/body/eval_jaxpr/ppermute | solution.py:19
  650.8 17.3 %collective-permute-done.1 = bf16[128,1024]{0,1:T(8,128)(2,1)} collective-permute-done((bf16[128,1024]{0,1:T(8,128)(2,1)S(1)}, bf16[128,1024]{0,1:T(8,128)(2,1)}, u32[]{:S(2)}, u32[]{:S(2)}) %collective-permute-start.1) | collective-permute-done | bytes 262176 | tf_op jit(solution)/shard_map/while/body/eval_jaxpr/ppermute | solution.py:19
  673.0 17.3 %collective-permute-done.1 = bf16[128,1024]{0,1:T(8,128)(2,1)} collective-permute-done((bf16[128,1024]{0,1:T(8,128)(2,1)S(1)}, bf16[128,1024]{0,1:T(8,128)(2,1)}, u32[]{:S(2)}, u32[]{:S(2)}) %collective-permute-start.1) | collective-permute-done | bytes 262176 | tf_op jit(solution)/shard_map/while/body/eval_jaxpr/ppermute | solution.py:19
  695.2 17.3 %collective-permute-done.1 = bf16[128,1024]{0,1:T(8,128)(2,1)} collective-permute-done((bf16[128,1024]{0,1:T(8,128)(2,1)S(1)}, bf16[128,1024]{0,1:T(8,128)(2,1)}, u32[]{:S(2)}, u32[]{:S(2)}) %collective-permute-start.1) | collective-permute-done | bytes 262176 | tf_op jit(solution)/shard_map/while/body/eval_jaxpr/ppermute | solution.py:19
  717.4 17.3 %collective-permute-done.1 = bf16[128,1024]{0,1:T(8,128)(2,1)} collective-permute-done((bf16[128,1024]{0,1:T(8,128)(2,1)S(1)}, bf16[128,1024]{0,1:T(8,128)(2,1)}, u32[]{:S(2)}, u32[]{:S(2)}) %collective-permute-start.1) | collective-permute-done | bytes 262176 | tf_op jit(solution)/shard_map/while/body/eval_jaxpr/ppermute | solution.py:19
  739.6 17.3 %collective-permute-done.1 = bf16[128,1024]{0,1:T(8,128)(2,1)} collective-permute-done((bf16[128,1024]{0,1:T(8,128)(2,1)S(1)}, bf16[128,1024]{0,1:T(8,128)(2,1)}, u32[]{:S(2)}, u32[]{:S(2)}) %collective-permute-start.1) | collective-permute-done | bytes 262176 | tf_op jit(solution)/shard_map/while/body/eval_jaxpr/ppermute | solution.py:19
  761.7 17.3 %collective-permute-done.1 = bf16[128,1024]{0,1:T(8,128)(2,1)} collective-permute-done((bf16[128,1024]{0,1:T(8,128)(2,1)S(1)}, bf16[128,1024]{0,1:T(8,128)(2,1)}, u32[]{:S(2)}, u32[]{:S(2)}) %collective-permute-start.1) | collective-permute-done | bytes 262176 | tf_op jit(solution)/shard_map/while/body/eval_jaxpr/ppermute | solution.py:19
  783.9 17.3 %collective-permute-done.1 = bf16[128,1024]{0,1:T(8,128)(2,1)} collective-permute-done((bf16[128,1024]{0,1:T(8,128)(2,1)S(1)}, bf16[128,1024]{0,1:T(8,128)(2,1)}, u32[]{:S(2)}, u32[]{:S(2)}) %collective-permute-start.1) | collective-permute-done | bytes 262176 | tf_op jit(solution)/shard_map/while/body/eval_jaxpr/ppermute | solution.py:19
  806.1 17.3 %collective-permute-done.1 = bf16[128,1024]{0,1:T(8,128)(2,1)} collective-permute-done((bf16[128,1024]{0,1:T(8,128)(2,1)S(1)}, bf16[128,1024]{0,1:T(8,128)(2,1)}, u32[]{:S(2)}, u32[]{:S(2)}) %collective-permute-start.1) | collective-permute-done | bytes 262176 | tf_op jit(solution)/shard_map/while/body/eval_jaxpr/ppermute | solution.py:19
  828.3 17.3 %collective-permute-done.1 = bf16[128,1024]{0,1:T(8,128)(2,1)} collective-permute-done((bf16[128,1024]{0,1:T(8,128)(2,1)S(1)}, bf16[128,1024]{0,1:T(8,128)(2,1)}, u32[]{:S(2)}, u32[]{:S(2)}) %collective-permute-start.1) | collective-permute-done | bytes 262176 | tf_op jit(solution)/shard_map/while/body/eval_jaxpr/ppermute | solution.py:19
  850.5 17.3 %collective-permute-done.1 = bf16[128,1024]{0,1:T(8,128)(2,1)} collective-permute-done((bf16[128,1024]{0,1:T(8,128)(2,1)S(1)}, bf16[128,1024]{0,1:T(8,128)(2,1)}, u32[]{:S(2)}, u32[]{:S(2)}) %collective-permute-start.1) | collective-permute-done | bytes 262176 | tf_op jit(solution)/shard_map/while/body/eval_jaxpr/ppermute | solution.py:19
  873.1 8.1 convolution_bitcast_fusion
  881.2 17.4 %copy.98 = f32[4096,1024]{1,0:T(8,128)} copy(f32[4096,1024]{0,1:T(8,128)} %convolution_bitcast_fusion) | data formatting | bytes 33554432
  898.6 2.2 copy.107
  900.8 3.8 copy.78
  904.6 4.2 broadcast_in_dim_reshape.3
  908.8 2.6 multiply_convert_fusion
  911.4 2.7 copy.119
  914.1 4.2 convert_element_type.98
  918.2 7.2 fusion.22
  925.5 635.5 %reduce-scatter.4.cloned.1.call-done = f32[32,1024]{1,0:T(8,128)} async-done(((f32[4096,1024]{1,0:T(8,128)}), f32[32,1024]{1,0:T(8,128)}) %reduce-scatter.4.cloned.1.call-update) | async-done | bytes 131088
  (274 shorter events, 125.0 us)
Async XLA Ops:
  7.2 208.4 %copy-start = (bf16[1,128,4096]{2,1,0:T(8,128)(2,1)S(1)}, bf16[1,128,4096]{2,1,0:T(8,128)(2,1)}, u32[]{:S(2)}) copy-start(bf16[1,128,4096]{2,1,0:T(8,128)(2,1)} %param.12) | copy-start | bytes 3145732
  7.2 208.4 %all-gather.2.cloned.1.call-start = ((), (), s32[]{:S(2)}) async-start(), calls=%async_computation.1 | async-start | bytes 8454144 | tf_op jit(solution)/shard_map/all_gather | solution.py:64
  7.9 1553.0 %reduce-scatter.4.cloned.1.call-start = ((), (), s32[]{:S(2)}) async-start(), calls=%async_computation.2 | async-start | bytes 16908288
  32.5 190.6 %copy-start.10 = (f32[128,64]{1,0:T(8,128)}, f32[128,64]{1,0:T(8,128)S(1)}, u32[]{:S(2)}) copy-start(f32[128,64]{1,0:T(8,128)S(1)} %get-tuple-element.695) | copy-start | bytes 98308
  32.5 190.5 %copy-start.11 = (f32[128,64]{1,0:T(8,128)}, f32[128,64]{1,0:T(8,128)S(1)}, u32[]{:S(2)}) copy-start(f32[128,64]{1,0:T(8,128)S(1)} %get-tuple-element.696) | copy-start | bytes 98308
  220.2 0.8 copy-start.7
  228.6 2.9 copy-start.8
  234.7 0.9 copy-start.9
  235.7 2.0 copy-start.6
  237.7 2.7 collective-permute-start
  241.1 16.7 %collective-permute-start = (bf16[128,1024]{0,1:T(8,128)(2,1)}, bf16[128,1024]{0,1:T(8,128)(2,1)S(1)}, u32[]{:S(2)}, u32[]{:S(2)}) collective-permute-start(bf16[128,1024]{0,1:T(8,128)(2,1)} %get-tuple-element.838), channel_id=1, source_target_pairs={{0,1},{1,2},{2,3},{3,4},{4,5},{5,6},{6,7},{7,8},{8,9},{9,10},{10,1... | collective-permute-start | bytes 786440 | tf_op jit(solution)/shard_map/while/body/eval_jaxpr/ppermute | solution.py:13
  258.4 7.9 collective-permute-start
  267.0 17.5 %collective-permute-start = (bf16[128,1024]{0,1:T(8,128)(2,1)}, bf16[128,1024]{0,1:T(8,128)(2,1)S(1)}, u32[]{:S(2)}, u32[]{:S(2)}) collective-permute-start(bf16[128,1024]{0,1:T(8,128)(2,1)} %get-tuple-element.838), channel_id=1, source_target_pairs={{0,1},{1,2},{2,3},{3,4},{4,5},{5,6},{6,7},{7,8},{8,9},{9,10},{10,1... | collective-permute-start | bytes 786440 | tf_op jit(solution)/shard_map/while/body/eval_jaxpr/ppermute | solution.py:13
  285.3 7.9 collective-permute-start
  293.9 13.9 collective-permute-start
  308.4 8.8 collective-permute-start
  318.0 18.4 %collective-permute-start = (bf16[128,1024]{0,1:T(8,128)(2,1)}, bf16[128,1024]{0,1:T(8,128)(2,1)S(1)}, u32[]{:S(2)}, u32[]{:S(2)}) collective-permute-start(bf16[128,1024]{0,1:T(8,128)(2,1)} %get-tuple-element.838), channel_id=1, source_target_pairs={{0,1},{1,2},{2,3},{3,4},{4,5},{5,6},{6,7},{7,8},{8,9},{9,10},{10,1... | collective-permute-start | bytes 786440 | tf_op jit(solution)/shard_map/while/body/eval_jaxpr/ppermute | solution.py:13
  337.1 8.8 collective-permute-start
  346.6 8.8 collective-permute-start
  356.1 8.8 collective-permute-start
  365.6 15.0 collective-permute-start
  381.3 8.8 collective-permute-start
  390.8 16.7 %collective-permute-start = (bf16[128,1024]{0,1:T(8,128)(2,1)}, bf16[128,1024]{0,1:T(8,128)(2,1)S(1)}, u32[]{:S(2)}, u32[]{:S(2)}) collective-permute-start(bf16[128,1024]{0,1:T(8,128)(2,1)} %get-tuple-element.838), channel_id=1, source_target_pairs={{0,1},{1,2},{2,3},{3,4},{4,5},{5,6},{6,7},{7,8},{8,9},{9,10},{10,1... | collective-permute-start | bytes 786440 | tf_op jit(solution)/shard_map/while/body/eval_jaxpr/ppermute | solution.py:13
  408.2 8.8 collective-permute-start
  431.1 2.8 copy-start.1
  435.4 3.0 copy-start.4
  440.6 1.9 copy-start.5
  443.6 100.2 %collective-permute-start.1 = (bf16[128,1024]{0,1:T(8,128)(2,1)S(1)}, bf16[128,1024]{0,1:T(8,128)(2,1)}, u32[]{:S(2)}, u32[]{:S(2)}) collective-permute-start(bf16[128,1024]{0,1:T(8,128)(2,1)S(1)} %convert_element_type.130), channel_id=1, source_target_pairs={{0,1},{1,2},{2,3},{3,4},{4,5},{5,6},{6,7},{7,8},{8,9},{9,10},{10,1... | collective-permute-start | bytes 786440 | tf_op jit(solution)/shard_map/while/body/eval_jaxpr/ppermute | solution.py:19
  548.6 14.8 collective-permute-start.1
  568.2 14.8 collective-permute-start.1
  587.8 14.8 collective-permute-start.1
  607.4 16.3 %collective-permute-start.1 = (bf16[128,1024]{0,1:T(8,128)(2,1)S(1)}, bf16[128,1024]{0,1:T(8,128)(2,1)}, u32[]{:S(2)}, u32[]{:S(2)}) collective-permute-start(bf16[128,1024]{0,1:T(8,128)(2,1)S(1)} %convert_element_type.130), channel_id=1, source_target_pairs={{0,1},{1,2},{2,3},{3,4},{4,5},{5,6},{6,7},{7,8},{8,9},{9,10},{10,1... | collective-permute-start | bytes 786440 | tf_op jit(solution)/shard_map/while/body/eval_jaxpr/ppermute | solution.py:19
  628.5 17.4 %collective-permute-start.1 = (bf16[128,1024]{0,1:T(8,128)(2,1)S(1)}, bf16[128,1024]{0,1:T(8,128)(2,1)}, u32[]{:S(2)}, u32[]{:S(2)}) collective-permute-start(bf16[128,1024]{0,1:T(8,128)(2,1)S(1)} %convert_element_type.130), channel_id=1, source_target_pairs={{0,1},{1,2},{2,3},{3,4},{4,5},{5,6},{6,7},{7,8},{8,9},{9,10},{10,1... | collective-permute-start | bytes 786440 | tf_op jit(solution)/shard_map/while/body/eval_jaxpr/ppermute | solution.py:19
  650.7 17.4 %collective-permute-start.1 = (bf16[128,1024]{0,1:T(8,128)(2,1)S(1)}, bf16[128,1024]{0,1:T(8,128)(2,1)}, u32[]{:S(2)}, u32[]{:S(2)}) collective-permute-start(bf16[128,1024]{0,1:T(8,128)(2,1)S(1)} %convert_element_type.130), channel_id=1, source_target_pairs={{0,1},{1,2},{2,3},{3,4},{4,5},{5,6},{6,7},{7,8},{8,9},{9,10},{10,1... | collective-permute-start | bytes 786440 | tf_op jit(solution)/shard_map/while/body/eval_jaxpr/ppermute | solution.py:19
  672.9 17.4 %collective-permute-start.1 = (bf16[128,1024]{0,1:T(8,128)(2,1)S(1)}, bf16[128,1024]{0,1:T(8,128)(2,1)}, u32[]{:S(2)}, u32[]{:S(2)}) collective-permute-start(bf16[128,1024]{0,1:T(8,128)(2,1)S(1)} %convert_element_type.130), channel_id=1, source_target_pairs={{0,1},{1,2},{2,3},{3,4},{4,5},{5,6},{6,7},{7,8},{8,9},{9,10},{10,1... | collective-permute-start | bytes 786440 | tf_op jit(solution)/shard_map/while/body/eval_jaxpr/ppermute | solution.py:19
  695.1 17.4 %collective-permute-start.1 = (bf16[128,1024]{0,1:T(8,128)(2,1)S(1)}, bf16[128,1024]{0,1:T(8,128)(2,1)}, u32[]{:S(2)}, u32[]{:S(2)}) collective-permute-start(bf16[128,1024]{0,1:T(8,128)(2,1)S(1)} %convert_element_type.130), channel_id=1, source_target_pairs={{0,1},{1,2},{2,3},{3,4},{4,5},{5,6},{6,7},{7,8},{8,9},{9,10},{10,1... | collective-permute-start | bytes 786440 | tf_op jit(solution)/shard_map/while/body/eval_jaxpr/ppermute | solution.py:19
  717.3 17.4 %collective-permute-start.1 = (bf16[128,1024]{0,1:T(8,128)(2,1)S(1)}, bf16[128,1024]{0,1:T(8,128)(2,1)}, u32[]{:S(2)}, u32[]{:S(2)}) collective-permute-start(bf16[128,1024]{0,1:T(8,128)(2,1)S(1)} %convert_element_type.130), channel_id=1, source_target_pairs={{0,1},{1,2},{2,3},{3,4},{4,5},{5,6},{6,7},{7,8},{8,9},{9,10},{10,1... | collective-permute-start | bytes 786440 | tf_op jit(solution)/shard_map/while/body/eval_jaxpr/ppermute | solution.py:19
  739.5 17.4 %collective-permute-start.1 = (bf16[128,1024]{0,1:T(8,128)(2,1)S(1)}, bf16[128,1024]{0,1:T(8,128)(2,1)}, u32[]{:S(2)}, u32[]{:S(2)}) collective-permute-start(bf16[128,1024]{0,1:T(8,128)(2,1)S(1)} %convert_element_type.130), channel_id=1, source_target_pairs={{0,1},{1,2},{2,3},{3,4},{4,5},{5,6},{6,7},{7,8},{8,9},{9,10},{10,1... | collective-permute-start | bytes 786440 | tf_op jit(solution)/shard_map/while/body/eval_jaxpr/ppermute | solution.py:19
  761.7 17.4 %collective-permute-start.1 = (bf16[128,1024]{0,1:T(8,128)(2,1)S(1)}, bf16[128,1024]{0,1:T(8,128)(2,1)}, u32[]{:S(2)}, u32[]{:S(2)}) collective-permute-start(bf16[128,1024]{0,1:T(8,128)(2,1)S(1)} %convert_element_type.130), channel_id=1, source_target_pairs={{0,1},{1,2},{2,3},{3,4},{4,5},{5,6},{6,7},{7,8},{8,9},{9,10},{10,1... | collective-permute-start | bytes 786440 | tf_op jit(solution)/shard_map/while/body/eval_jaxpr/ppermute | solution.py:19
  783.9 17.4 %collective-permute-start.1 = (bf16[128,1024]{0,1:T(8,128)(2,1)S(1)}, bf16[128,1024]{0,1:T(8,128)(2,1)}, u32[]{:S(2)}, u32[]{:S(2)}) collective-permute-start(bf16[128,1024]{0,1:T(8,128)(2,1)S(1)} %convert_element_type.130), channel_id=1, source_target_pairs={{0,1},{1,2},{2,3},{3,4},{4,5},{5,6},{6,7},{7,8},{8,9},{9,10},{10,1... | collective-permute-start | bytes 786440 | tf_op jit(solution)/shard_map/while/body/eval_jaxpr/ppermute | solution.py:19
  806.0 17.4 %collective-permute-start.1 = (bf16[128,1024]{0,1:T(8,128)(2,1)S(1)}, bf16[128,1024]{0,1:T(8,128)(2,1)}, u32[]{:S(2)}, u32[]{:S(2)}) collective-permute-start(bf16[128,1024]{0,1:T(8,128)(2,1)S(1)} %convert_element_type.130), channel_id=1, source_target_pairs={{0,1},{1,2},{2,3},{3,4},{4,5},{5,6},{6,7},{7,8},{8,9},{9,10},{10,1... | collective-permute-start | bytes 786440 | tf_op jit(solution)/shard_map/while/body/eval_jaxpr/ppermute | solution.py:19
  828.2 17.4 %collective-permute-start.1 = (bf16[128,1024]{0,1:T(8,128)(2,1)S(1)}, bf16[128,1024]{0,1:T(8,128)(2,1)}, u32[]{:S(2)}, u32[]{:S(2)}) collective-permute-start(bf16[128,1024]{0,1:T(8,128)(2,1)S(1)} %convert_element_type.130), channel_id=1, source_target_pairs={{0,1},{1,2},{2,3},{3,4},{4,5},{5,6},{6,7},{7,8},{8,9},{9,10},{10,1... | collective-permute-start | bytes 786440 | tf_op jit(solution)/shard_map/while/body/eval_jaxpr/ppermute | solution.py:19
  850.4 17.4 %collective-permute-start.1 = (bf16[128,1024]{0,1:T(8,128)(2,1)S(1)}, bf16[128,1024]{0,1:T(8,128)(2,1)}, u32[]{:S(2)}, u32[]{:S(2)}) collective-permute-start(bf16[128,1024]{0,1:T(8,128)(2,1)S(1)} %convert_element_type.130), channel_id=1, source_target_pairs={{0,1},{1,2},{2,3},{3,4},{4,5},{5,6},{6,7},{7,8},{8,9},{9,10},{10,1... | collective-permute-start | bytes 786440 | tf_op jit(solution)/shard_map/while/body/eval_jaxpr/ppermute | solution.py:19
Sparse Core Ops, SparseCore 0:
  9.7 205.8 all-gather.1
  898.7 662.1 reduce-scatter.3
where the time goes:
time: 1570 us
  waiting for transfers between devices  1170 us (75%)
  starting transfers between devices  166 us (11%)
  local copies, waits for them, and re-layouts  91.6 us (6%)
  other arithmetic  90.5 us (6%)
  matrix products  31.1 us (2%)
    unnamed x3, waiting for transfers between devices  636 us
    ppermute x16, waiting for transfers between devices, shifted_2(): return lax.ppermute(value, axis, pairs)  336 us
    all_gather x1, waiting for transfers between devices, on_device(): weight_all = lax.all_gather(kv_weight, ('dp', 'ctx'), axis=0, tiled=True)  182 us
    ppermute x15, starting transfers between devices, shifted(): return lax.ppermute(block, axis, route)  149 us
    unnamed x22, local copies, waits for them, and re-layouts  32.2 us
  transfers between devices with their start and end apart: 33, of which 33 were waited for; matrix products, arithmetic and copies ran while one was open for 3% of the time, Pallas kernels for 0%

commit v1 on v0

--- a/solution.py
+++ b/solution.py
@@ -5,6 +5,11 @@
 
 DH = 128
 ROPE_BASE = 500000.0
+
+
+def exchange_gather(x, axis, dim):
+    repeated = jnp.stack([x] * lax.axis_size(axis))
+    return jnp.concatenate(lax.all_to_all(repeated, axis, 0, 0), axis=dim)
 
 
 def shifted(block, axis, distance):
@@ -61,7 +66,7 @@
     ctx_index = lax.axis_index("ctx")
     score_scale = head_dim ** (-0.5)
     tokens = inputs[0]
-    weight_all = lax.all_gather(kv_weight, ("dp", "ctx"), axis=0, tiled=True)
+    weight_all = exchange_gather(kv_weight, ("dp", "ctx"), 0)
     projected = jnp.dot(tokens, weight_all, preferred_element_type=jnp.float32)
     positions = ctx_index * token_count + jnp.arange(token_count, dtype=jnp.int32)
     key_rows = rotary(

time: 1570 us -> 1490 us (0.949)
  waiting for transfers between devices: 1170 us -> 1060 us
  starting transfers between devices: 166 us -> 188 us
    all_gather x1 -> x0, waiting for transfers between devices: 182 us -> none  [on_device(): weight_all = lax.all_gather(kv_weight, ('dp', 'ctx'), axis=0, tiled=True)]
    all_to_all x0 -> x1, waiting for transfers between devices: none -> 75.7 us  [exchange_gather(): return jnp.concatenate(lax.all_to_all(repeated, axis, 0, 0), axis=dim)]
    unnamed x3 -> x2, waiting for transfers between devices: 636 us -> 635 us
  transfers between devices with their start and end apart: 33 -> 33, of which waited for: 33 -> 33; matrix products, arithmetic and copies ran while one was open for 3% -> 4% of each run, Pallas kernels for 0% -> 0%
where the time goes in v1:
time: 1490 us; the launch traced here: 1480 us
  waiting for transfers between devices  1060 us (71%)
  starting transfers between devices  188 us (13%)
  local copies, waits for them, and re-layouts  96.8 us (6%)
  other arithmetic  90.4 us (6%)
  matrix products  31.2 us (2%)
    unnamed x2, waiting for transfers between devices  635 us
    ppermute x16, waiting for transfers between devices, shifted_2(): return lax.ppermute(value, axis, pairs)  333 us
    ppermute x15, starting transfers between devices, shifted(): return lax.ppermute(block, axis, route)  160 us
    all_to_all x1, waiting for transfers between devices, exchange_gather(): return jnp.concatenate(lax.all_to_all(repeated, axis, 0, 0), axis=dim)  75.7 us
    unnamed x22, local copies, waits for them, and re-layouts  32.1 us
  transfers between devices with their start and end apart: 33, of which 33 were waited for; matrix products, arithmetic and copies ran while one was open for 4% of the time, Pallas kernels for 0%

profile of v1, /device:TPU:0, one launch (start us, length us, event | category | flops | bytes accessed | tf_op | source)
XLA Modules:
  0.0 1484.0 jit_solution(11157764345537505490)
XLA Ops:
  7.2 5.2 stack.2
  12.4 11.7 all-to-all-start
  24.2 2.2 copy.106
  26.4 3.8 copy.71
  30.2 2.8 reshape.240
  33.0 2.5 copy.76
  35.5 3.5 copy.108
  39.0 5.1 copy.79
  44.2 4.2 reshape.243
  49.5 75.7 %all-to-all-done = bf16[128,32,1024]{2,1,0:T(8,128)(2,1)} async-done(((bf16[128,32,1024]{2,1,0:T(8,128)(2,1)}), bf16[128,32,1024]{2,1,0:T(8,128)(2,1)}, u32[]{:S(2)}, u32[]{:S(2)}) %all-to-all-start) | async-done | bytes 8388640 | tf_op jit(solution)/shard_map/all_to_all | solution.py:12
  125.2 4.6 fusion.28
  138.2 2.2 fusion.42
  141.0 3.3 convolution_add_fusion.1
  145.3 2.0 copy-done.6
  147.3 190.5 %while.38 = (s32[]{:T(128)}, bf16[128,1024]{0,1:T(8,128)(2,1)}, bf16[16,128,1024]{1,2,0:T(8,128)(2,1)}, f32[4,2048,1]{1,0,2:T(4,128)S(1)}, f32[4,2048,1]{1,0,2:T...) while((s32[]{:T(128)}, bf16[128,1024]{0,1:T(8,128)(2,1)}, ...), condition=%wide.region_7.8_spmd.clone, body=%wide.region_2.7_spmd.clone.sunk | while | flops 551063552 | bytes 61154760 | solution.py:154
  150.6 13.7 collective-permute-start
  166.4 6.5 collective-permute-start
  175.0 16.2 %collective-permute-start = (bf16[128,1024]{0,1:T(8,128)(2,1)}, bf16[128,1024]{0,1:T(8,128)(2,1)S(1)}, u32[]{:S(2)}, u32[]{:S(2)}) collective-permute-start(bf16[128,1024]{0,1:T(8,128)(2,1)} %get-tuple-element.838), channel_id=1, source_target_pairs={{0,1},{1,2},{2,3},{3,4},{4,5},{5,6},{6,7},{7,8},{8,9},{9,10},{10,1... | collective-permute-start | bytes 786440 | tf_op jit(solution)/shard_map/while/body/eval_jaxpr/ppermute | solution.py:18
  193.3 6.5 collective-permute-start
  201.8 15.8 %collective-permute-start = (bf16[128,1024]{0,1:T(8,128)(2,1)}, bf16[128,1024]{0,1:T(8,128)(2,1)S(1)}, u32[]{:S(2)}, u32[]{:S(2)}) collective-permute-start(bf16[128,1024]{0,1:T(8,128)(2,1)} %get-tuple-element.838), channel_id=1, source_target_pairs={{0,1},{1,2},{2,3},{3,4},{4,5},{5,6},{6,7},{7,8},{8,9},{9,10},{10,1... | collective-permute-start | bytes 786440 | tf_op jit(solution)/shard_map/while/body/eval_jaxpr/ppermute | solution.py:18
  219.7 7.4 collective-permute-start
  229.2 17.1 %collective-permute-start = (bf16[128,1024]{0,1:T(8,128)(2,1)}, bf16[128,1024]{0,1:T(8,128)(2,1)S(1)}, u32[]{:S(2)}, u32[]{:S(2)}) collective-permute-start(bf16[128,1024]{0,1:T(8,128)(2,1)} %get-tuple-element.838), channel_id=1, source_target_pairs={{0,1},{1,2},{2,3},{3,4},{4,5},{5,6},{6,7},{7,8},{8,9},{9,10},{10,1... | collective-permute-start | bytes 786440 | tf_op jit(solution)/shard_map/while/body/eval_jaxpr/ppermute | solution.py:18
  248.3 7.4 collective-permute-start
  257.8 11.1 collective-permute-start
  271.0 7.4 collective-permute-start
  280.5 17.1 %collective-permute-start = (bf16[128,1024]{0,1:T(8,128)(2,1)}, bf16[128,1024]{0,1:T(8,128)(2,1)S(1)}, u32[]{:S(2)}, u32[]{:S(2)}) collective-permute-start(bf16[128,1024]{0,1:T(8,128)(2,1)} %get-tuple-element.838), channel_id=1, source_target_pairs={{0,1},{1,2},{2,3},{3,4},{4,5},{5,6},{6,7},{7,8},{8,9},{9,10},{10,1... | collective-permute-start | bytes 786440 | tf_op jit(solution)/shard_map/while/body/eval_jaxpr/ppermute | solution.py:18
  299.6 7.4 collective-permute-start
  309.1 17.0 %collective-permute-start = (bf16[128,1024]{0,1:T(8,128)(2,1)}, bf16[128,1024]{0,1:T(8,128)(2,1)S(1)}, u32[]{:S(2)}, u32[]{:S(2)}) collective-permute-start(bf16[128,1024]{0,1:T(8,128)(2,1)} %get-tuple-element.838), channel_id=1, source_target_pairs={{0,1},{1,2},{2,3},{3,4},{4,5},{5,6},{6,7},{7,8},{8,9},{9,10},{10,1... | collective-permute-start | bytes 786440 | tf_op jit(solution)/shard_map/while/body/eval_jaxpr/ppermute | solution.py:18
  328.2 7.4 collective-permute-start
  337.7 5.4 copy.77
  343.2 5.0 multiply_reduce_fusion
  348.2 2.2 broadcast.184
  350.4 436.3 %while.39 = (s32[]{:T(128)}, f32[128,1024]{0,1:T(8,128)}, f32[4,2048,128]{2,1,0:T(8,128)}, s32[]{:T(128)}, bf16[16,128,1024]{1,2,0:T(8,128)(2,1)}, /*index=5*/bf...) while((s32[]{:T(128)}, f32[128,1024]{0,1:T(8,128)}, ...), condition=%wide.region_12.13_spmd.clone, body=%wide.region_9.12_spmd.clone.sunk | while | flops 1351823360 | bytes 85468640 | solution.py:214
  351.3 11.4 conditional.7
  356.3 2.2 maximum_add_fusion
  358.5 2.2 convolution_add_fusion
  360.7 1.9 copy-done.5
  363.7 15.2 %collective-permute-start.1 = (bf16[128,1024]{0,1:T(8,128)(2,1)S(1)}, bf16[128,1024]{0,1:T(8,128)(2,1)}, u32[]{:S(2)}, u32[]{:S(2)}) collective-permute-start(bf16[128,1024]{0,1:T(8,128)(2,1)S(1)} %convert_element_type.130), channel_id=1, source_target_pairs={{0,1},{1,2},{2,3},{3,4},{4,5},{5,6},{6,7},{7,8},{8,9},{9,10},{10,1... | collective-permute-start | bytes 786440 | tf_op jit(solution)/shard_map/while/body/eval_jaxpr/ppermute | solution.py:24
  379.0 82.2 %collective-permute-done.1 = bf16[128,1024]{0,1:T(8,128)(2,1)} collective-permute-done((bf16[128,1024]{0,1:T(8,128)(2,1)S(1)}, bf16[128,1024]{0,1:T(8,128)(2,1)}, u32[]{:S(2)}, u32[]{:S(2)}) %collective-permute-start.1) | collective-permute-done | bytes 262176 | tf_op jit(solution)/shard_map/while/body/eval_jaxpr/ppermute | solution.py:24
  466.1 14.7 collective-permute-done.1
  485.6 14.7 collective-permute-done.1
  505.2 14.7 collective-permute-done.1
  524.8 16.2 %collective-permute-done.1 = bf16[128,1024]{0,1:T(8,128)(2,1)} collective-permute-done((bf16[128,1024]{0,1:T(8,128)(2,1)S(1)}, bf16[128,1024]{0,1:T(8,128)(2,1)}, u32[]{:S(2)}, u32[]{:S(2)}) %collective-permute-start.1) | collective-permute-done | bytes 262176 | tf_op jit(solution)/shard_map/while/body/eval_jaxpr/ppermute | solution.py:24
  545.9 17.3 %collective-permute-done.1 = bf16[128,1024]{0,1:T(8,128)(2,1)} collective-permute-done((bf16[128,1024]{0,1:T(8,128)(2,1)S(1)}, bf16[128,1024]{0,1:T(8,128)(2,1)}, u32[]{:S(2)}, u32[]{:S(2)}) %collective-permute-start.1) | collective-permute-done | bytes 262176 | tf_op jit(solution)/shard_map/while/body/eval_jaxpr/ppermute | solution.py:24
  568.1 17.3 %collective-permute-done.1 = bf16[128,1024]{0,1:T(8,128)(2,1)} collective-permute-done((bf16[128,1024]{0,1:T(8,128)(2,1)S(1)}, bf16[128,1024]{0,1:T(8,128)(2,1)}, u32[]{:S(2)}, u32[]{:S(2)}) %collective-permute-start.1) | collective-permute-done | bytes 262176 | tf_op jit(solution)/shard_map/while/body/eval_jaxpr/ppermute | solution.py:24
  590.2 17.3 %collective-permute-done.1 = bf16[128,1024]{0,1:T(8,128)(2,1)} collective-permute-done((bf16[128,1024]{0,1:T(8,128)(2,1)S(1)}, bf16[128,1024]{0,1:T(8,128)(2,1)}, u32[]{:S(2)}, u32[]{:S(2)}) %collective-permute-start.1) | collective-permute-done | bytes 262176 | tf_op jit(solution)/shard_map/while/body/eval_jaxpr/ppermute | solution.py:24
  612.4 17.3 %collective-permute-done.1 = bf16[128,1024]{0,1:T(8,128)(2,1)} collective-permute-done((bf16[128,1024]{0,1:T(8,128)(2,1)S(1)}, bf16[128,1024]{0,1:T(8,128)(2,1)}, u32[]{:S(2)}, u32[]{:S(2)}) %collective-permute-start.1) | collective-permute-done | bytes 262176 | tf_op jit(solution)/shard_map/while/body/eval_jaxpr/ppermute | solution.py:24
  634.6 17.3 %collective-permute-done.1 = bf16[128,1024]{0,1:T(8,128)(2,1)} collective-permute-done((bf16[128,1024]{0,1:T(8,128)(2,1)S(1)}, bf16[128,1024]{0,1:T(8,128)(2,1)}, u32[]{:S(2)}, u32[]{:S(2)}) %collective-permute-start.1) | collective-permute-done | bytes 262176 | tf_op jit(solution)/shard_map/while/body/eval_jaxpr/ppermute | solution.py:24
  656.8 17.3 %collective-permute-done.1 = bf16[128,1024]{0,1:T(8,128)(2,1)} collective-permute-done((bf16[128,1024]{0,1:T(8,128)(2,1)S(1)}, bf16[128,1024]{0,1:T(8,128)(2,1)}, u32[]{:S(2)}, u32[]{:S(2)}) %collective-permute-start.1) | collective-permute-done | bytes 262176 | tf_op jit(solution)/shard_map/while/body/eval_jaxpr/ppermute | solution.py:24
  678.9 17.3 %collective-permute-done.1 = bf16[128,1024]{0,1:T(8,128)(2,1)} collective-permute-done((bf16[128,1024]{0,1:T(8,128)(2,1)S(1)}, bf16[128,1024]{0,1:T(8,128)(2,1)}, u32[]{:S(2)}, u32[]{:S(2)}) %collective-permute-start.1) | collective-permute-done | bytes 262176 | tf_op jit(solution)/shard_map/while/body/eval_jaxpr/ppermute | solution.py:24
  701.1 17.3 %collective-permute-done.1 = bf16[128,1024]{0,1:T(8,128)(2,1)} collective-permute-done((bf16[128,1024]{0,1:T(8,128)(2,1)S(1)}, bf16[128,1024]{0,1:T(8,128)(2,1)}, u32[]{:S(2)}, u32[]{:S(2)}) %collective-permute-start.1) | collective-permute-done | bytes 262176 | tf_op jit(solution)/shard_map/while/body/eval_jaxpr/ppermute | solution.py:24
  723.3 17.3 %collective-permute-done.1 = bf16[128,1024]{0,1:T(8,128)(2,1)} collective-permute-done((bf16[128,1024]{0,1:T(8,128)(2,1)S(1)}, bf16[128,1024]{0,1:T(8,128)(2,1)}, u32[]{:S(2)}, u32[]{:S(2)}) %collective-permute-start.1) | collective-permute-done | bytes 262176 | tf_op jit(solution)/shard_map/while/body/eval_jaxpr/ppermute | solution.py:24
  745.4 17.3 %collective-permute-done.1 = bf16[128,1024]{0,1:T(8,128)(2,1)} collective-permute-done((bf16[128,1024]{0,1:T(8,128)(2,1)S(1)}, bf16[128,1024]{0,1:T(8,128)(2,1)}, u32[]{:S(2)}, u32[]{:S(2)}) %collective-permute-start.1) | collective-permute-done | bytes 262176 | tf_op jit(solution)/shard_map/while/body/eval_jaxpr/ppermute | solution.py:24
  767.6 17.3 %collective-permute-done.1 = bf16[128,1024]{0,1:T(8,128)(2,1)} collective-permute-done((bf16[128,1024]{0,1:T(8,128)(2,1)S(1)}, bf16[128,1024]{0,1:T(8,128)(2,1)}, u32[]{:S(2)}, u32[]{:S(2)}) %collective-permute-start.1) | collective-permute-done | bytes 262176 | tf_op jit(solution)/shard_map/while/body/eval_jaxpr/ppermute | solution.py:24
  790.2 8.1 convolution_bitcast_fusion
  798.2 17.4 %copy.98 = f32[4096,1024]{1,0:T(8,128)} copy(f32[4096,1024]{0,1:T(8,128)} %convolution_bitcast_fusion) | data formatting | bytes 33554432
  815.7 2.2 copy.107
  817.9 3.8 copy.78
  821.7 4.2 broadcast_in_dim_reshape.3
  825.8 2.6 multiply_convert_fusion
  828.5 2.7 copy.119
  831.2 4.2 convert_element_type.98
  835.3 7.3 fusion.22
  842.6 634.6 %reduce-scatter.4.cloned.1.call-done = f32[32,1024]{1,0:T(8,128)} async-done(((f32[4096,1024]{1,0:T(8,128)}), f32[32,1024]{1,0:T(8,128)}) %reduce-scatter.4.cloned.1.call-update) | async-done | bytes 131088
  (274 shorter events, 128.0 us)
Async XLA Ops:
  7.2 118.0 %copy-start = (bf16[1,128,4096]{2,1,0:T(8,128)(2,1)S(1)}, bf16[1,128,4096]{2,1,0:T(8,128)(2,1)}, u32[]{:S(2)}) copy-start(bf16[1,128,4096]{2,1,0:T(8,128)(2,1)} %param.12) | copy-start | bytes 3145732
  12.4 112.8 %all-to-all-start = ((bf16[128,32,1024]{2,1,0:T(8,128)(2,1)}), bf16[128,32,1024]{2,1,0:T(8,128)(2,1)}, u32[]{:S(2)}, u32[]{:S(2)}) async-start(bf16[128,32,1024]{2,1,0:T(8,128)(2,1)} %stack.2), calls=%async_computation | async-start | bytes 16777216 | tf_op jit(solution)/shard_map/all_to_all | solution.py:12
  24.1 1453.0 %reduce-scatter.4.cloned.1.call-start = ((), (), s32[]{:S(2)}) async-start(), calls=%async_computation.2 | async-start | bytes 16908288
  48.7 84.0 %copy-start.10 = (f32[128,64]{1,0:T(8,128)}, f32[128,64]{1,0:T(8,128)S(1)}, u32[]{:S(2)}) copy-start(f32[128,64]{1,0:T(8,128)S(1)} %get-tuple-element.695) | copy-start | bytes 98308
  48.7 84.0 %copy-start.11 = (f32[128,64]{1,0:T(8,128)}, f32[128,64]{1,0:T(8,128)S(1)}, u32[]{:S(2)}) copy-start(f32[128,64]{1,0:T(8,128)S(1)} %get-tuple-element.696) | copy-start | bytes 98308
  129.8 0.8 copy-start.7
  138.2 2.9 copy-start.8
  144.3 0.9 copy-start.9
  145.3 2.0 copy-start.6
  147.3 2.6 collective-permute-start
  150.6 15.1 %collective-permute-start = (bf16[128,1024]{0,1:T(8,128)(2,1)}, bf16[128,1024]{0,1:T(8,128)(2,1)S(1)}, u32[]{:S(2)}, u32[]{:S(2)}) collective-permute-start(bf16[128,1024]{0,1:T(8,128)(2,1)} %get-tuple-element.838), channel_id=1, source_target_pairs={{0,1},{1,2},{2,3},{3,4},{4,5},{5,6},{6,7},{7,8},{8,9},{9,10},{10,1... | collective-permute-start | bytes 786440 | tf_op jit(solution)/shard_map/while/body/eval_jaxpr/ppermute | solution.py:18
  166.4 7.9 collective-permute-start
  175.0 17.5 %collective-permute-start = (bf16[128,1024]{0,1:T(8,128)(2,1)}, bf16[128,1024]{0,1:T(8,128)(2,1)S(1)}, u32[]{:S(2)}, u32[]{:S(2)}) collective-permute-start(bf16[128,1024]{0,1:T(8,128)(2,1)} %get-tuple-element.838), channel_id=1, source_target_pairs={{0,1},{1,2},{2,3},{3,4},{4,5},{5,6},{6,7},{7,8},{8,9},{9,10},{10,1... | collective-permute-start | bytes 786440 | tf_op jit(solution)/shard_map/while/body/eval_jaxpr/ppermute | solution.py:18
  193.3 7.9 collective-permute-start
  201.8 17.2 %collective-permute-start = (bf16[128,1024]{0,1:T(8,128)(2,1)}, bf16[128,1024]{0,1:T(8,128)(2,1)S(1)}, u32[]{:S(2)}, u32[]{:S(2)}) collective-permute-start(bf16[128,1024]{0,1:T(8,128)(2,1)} %get-tuple-element.838), channel_id=1, source_target_pairs={{0,1},{1,2},{2,3},{3,4},{4,5},{5,6},{6,7},{7,8},{8,9},{9,10},{10,1... | collective-permute-start | bytes 786440 | tf_op jit(solution)/shard_map/while/body/eval_jaxpr/ppermute | solution.py:18
  219.7 8.8 collective-permute-start
  229.2 18.4 %collective-permute-start = (bf16[128,1024]{0,1:T(8,128)(2,1)}, bf16[128,1024]{0,1:T(8,128)(2,1)S(1)}, u32[]{:S(2)}, u32[]{:S(2)}) collective-permute-start(bf16[128,1024]{0,1:T(8,128)(2,1)} %get-tuple-element.838), channel_id=1, source_target_pairs={{0,1},{1,2},{2,3},{3,4},{4,5},{5,6},{6,7},{7,8},{8,9},{9,10},{10,1... | collective-permute-start | bytes 786440 | tf_op jit(solution)/shard_map/while/body/eval_jaxpr/ppermute | solution.py:18
  248.3 8.8 collective-permute-start
  257.8 12.5 collective-permute-start
  271.0 8.8 collective-permute-start
  280.5 18.4 %collective-permute-start = (bf16[128,1024]{0,1:T(8,128)(2,1)}, bf16[128,1024]{0,1:T(8,128)(2,1)S(1)}, u32[]{:S(2)}, u32[]{:S(2)}) collective-permute-start(bf16[128,1024]{0,1:T(8,128)(2,1)} %get-tuple-element.838), channel_id=1, source_target_pairs={{0,1},{1,2},{2,3},{3,4},{4,5},{5,6},{6,7},{7,8},{8,9},{9,10},{10,1... | collective-permute-start | bytes 786440 | tf_op jit(solution)/shard_map/while/body/eval_jaxpr/ppermute | solution.py:18
  299.6 8.8 collective-permute-start
  309.1 18.4 %collective-permute-start = (bf16[128,1024]{0,1:T(8,128)(2,1)}, bf16[128,1024]{0,1:T(8,128)(2,1)S(1)}, u32[]{:S(2)}, u32[]{:S(2)}) collective-permute-start(bf16[128,1024]{0,1:T(8,128)(2,1)} %get-tuple-element.838), channel_id=1, source_target_pairs={{0,1},{1,2},{2,3},{3,4},{4,5},{5,6},{6,7},{7,8},{8,9},{9,10},{10,1... | collective-permute-start | bytes 786440 | tf_op jit(solution)/shard_map/while/body/eval_jaxpr/ppermute | solution.py:18
  328.2 8.8 collective-permute-start
  351.3 2.8 copy-start.1
  355.6 3.0 copy-start.4
  360.7 1.9 copy-start.5
  363.7 97.5 %collective-permute-start.1 = (bf16[128,1024]{0,1:T(8,128)(2,1)S(1)}, bf16[128,1024]{0,1:T(8,128)(2,1)}, u32[]{:S(2)}, u32[]{:S(2)}) collective-permute-start(bf16[128,1024]{0,1:T(8,128)(2,1)S(1)} %convert_element_type.130), channel_id=1, source_target_pairs={{0,1},{1,2},{2,3},{3,4},{4,5},{5,6},{6,7},{7,8},{8,9},{9,10},{10,1... | collective-permute-start | bytes 786440 | tf_op jit(solution)/shard_map/while/body/eval_jaxpr/ppermute | solution.py:24
  466.0 14.8 collective-permute-start.1
  485.6 14.8 collective-permute-start.1
  505.1 14.8 collective-permute-start.1
  524.7 16.3 %collective-permute-start.1 = (bf16[128,1024]{0,1:T(8,128)(2,1)S(1)}, bf16[128,1024]{0,1:T(8,128)(2,1)}, u32[]{:S(2)}, u32[]{:S(2)}) collective-permute-start(bf16[128,1024]{0,1:T(8,128)(2,1)S(1)} %convert_element_type.130), channel_id=1, source_target_pairs={{0,1},{1,2},{2,3},{3,4},{4,5},{5,6},{6,7},{7,8},{8,9},{9,10},{10,1... | collective-permute-start | bytes 786440 | tf_op jit(solution)/shard_map/while/body/eval_jaxpr/ppermute | solution.py:24
  545.8 17.4 %collective-permute-start.1 = (bf16[128,1024]{0,1:T(8,128)(2,1)S(1)}, bf16[128,1024]{0,1:T(8,128)(2,1)}, u32[]{:S(2)}, u32[]{:S(2)}) collective-permute-start(bf16[128,1024]{0,1:T(8,128)(2,1)S(1)} %convert_element_type.130), channel_id=1, source_target_pairs={{0,1},{1,2},{2,3},{3,4},{4,5},{5,6},{6,7},{7,8},{8,9},{9,10},{10,1... | collective-permute-start | bytes 786440 | tf_op jit(solution)/shard_map/while/body/eval_jaxpr/ppermute | solution.py:24
  568.0 17.4 %collective-permute-start.1 = (bf16[128,1024]{0,1:T(8,128)(2,1)S(1)}, bf16[128,1024]{0,1:T(8,128)(2,1)}, u32[]{:S(2)}, u32[]{:S(2)}) collective-permute-start(bf16[128,1024]{0,1:T(8,128)(2,1)S(1)} %convert_element_type.130), channel_id=1, source_target_pairs={{0,1},{1,2},{2,3},{3,4},{4,5},{5,6},{6,7},{7,8},{8,9},{9,10},{10,1... | collective-permute-start | bytes 786440 | tf_op jit(solution)/shard_map/while/body/eval_jaxpr/ppermute | solution.py:24
  590.2 17.4 %collective-permute-start.1 = (bf16[128,1024]{0,1:T(8,128)(2,1)S(1)}, bf16[128,1024]{0,1:T(8,128)(2,1)}, u32[]{:S(2)}, u32[]{:S(2)}) collective-permute-start(bf16[128,1024]{0,1:T(8,128)(2,1)S(1)} %convert_element_type.130), channel_id=1, source_target_pairs={{0,1},{1,2},{2,3},{3,4},{4,5},{5,6},{6,7},{7,8},{8,9},{9,10},{10,1... | collective-permute-start | bytes 786440 | tf_op jit(solution)/shard_map/while/body/eval_jaxpr/ppermute | solution.py:24
  612.3 17.4 %collective-permute-start.1 = (bf16[128,1024]{0,1:T(8,128)(2,1)S(1)}, bf16[128,1024]{0,1:T(8,128)(2,1)}, u32[]{:S(2)}, u32[]{:S(2)}) collective-permute-start(bf16[128,1024]{0,1:T(8,128)(2,1)S(1)} %convert_element_type.130), channel_id=1, source_target_pairs={{0,1},{1,2},{2,3},{3,4},{4,5},{5,6},{6,7},{7,8},{8,9},{9,10},{10,1... | collective-permute-start | bytes 786440 | tf_op jit(solution)/shard_map/while/body/eval_jaxpr/ppermute | solution.py:24
  634.5 17.4 %collective-permute-start.1 = (bf16[128,1024]{0,1:T(8,128)(2,1)S(1)}, bf16[128,1024]{0,1:T(8,128)(2,1)}, u32[]{:S(2)}, u32[]{:S(2)}) collective-permute-start(bf16[128,1024]{0,1:T(8,128)(2,1)S(1)} %convert_element_type.130), channel_id=1, source_target_pairs={{0,1},{1,2},{2,3},{3,4},{4,5},{5,6},{6,7},{7,8},{8,9},{9,10},{10,1... | collective-permute-start | bytes 786440 | tf_op jit(solution)/shard_map/while/body/eval_jaxpr/ppermute | solution.py:24
  656.7 17.4 %collective-permute-start.1 = (bf16[128,1024]{0,1:T(8,128)(2,1)S(1)}, bf16[128,1024]{0,1:T(8,128)(2,1)}, u32[]{:S(2)}, u32[]{:S(2)}) collective-permute-start(bf16[128,1024]{0,1:T(8,128)(2,1)S(1)} %convert_element_type.130), channel_id=1, source_target_pairs={{0,1},{1,2},{2,3},{3,4},{4,5},{5,6},{6,7},{7,8},{8,9},{9,10},{10,1... | collective-permute-start | bytes 786440 | tf_op jit(solution)/shard_map/while/body/eval_jaxpr/ppermute | solution.py:24
  678.8 17.4 %collective-permute-start.1 = (bf16[128,1024]{0,1:T(8,128)(2,1)S(1)}, bf16[128,1024]{0,1:T(8,128)(2,1)}, u32[]{:S(2)}, u32[]{:S(2)}) collective-permute-start(bf16[128,1024]{0,1:T(8,128)(2,1)S(1)} %convert_element_type.130), channel_id=1, source_target_pairs={{0,1},{1,2},{2,3},{3,4},{4,5},{5,6},{6,7},{7,8},{8,9},{9,10},{10,1... | collective-permute-start | bytes 786440 | tf_op jit(solution)/shard_map/while/body/eval_jaxpr/ppermute | solution.py:24
  701.0 17.4 %collective-permute-start.1 = (bf16[128,1024]{0,1:T(8,128)(2,1)S(1)}, bf16[128,1024]{0,1:T(8,128)(2,1)}, u32[]{:S(2)}, u32[]{:S(2)}) collective-permute-start(bf16[128,1024]{0,1:T(8,128)(2,1)S(1)} %convert_element_type.130), channel_id=1, source_target_pairs={{0,1},{1,2},{2,3},{3,4},{4,5},{5,6},{6,7},{7,8},{8,9},{9,10},{10,1... | collective-permute-start | bytes 786440 | tf_op jit(solution)/shard_map/while/body/eval_jaxpr/ppermute | solution.py:24
  723.2 17.4 %collective-permute-start.1 = (bf16[128,1024]{0,1:T(8,128)(2,1)S(1)}, bf16[128,1024]{0,1:T(8,128)(2,1)}, u32[]{:S(2)}, u32[]{:S(2)}) collective-permute-start(bf16[128,1024]{0,1:T(8,128)(2,1)S(1)} %convert_element_type.130), channel_id=1, source_target_pairs={{0,1},{1,2},{2,3},{3,4},{4,5},{5,6},{6,7},{7,8},{8,9},{9,10},{10,1... | collective-permute-start | bytes 786440 | tf_op jit(solution)/shard_map/while/body/eval_jaxpr/ppermute | solution.py:24
  745.4 17.4 %collective-permute-start.1 = (bf16[128,1024]{0,1:T(8,128)(2,1)S(1)}, bf16[128,1024]{0,1:T(8,128)(2,1)}, u32[]{:S(2)}, u32[]{:S(2)}) collective-permute-start(bf16[128,1024]{0,1:T(8,128)(2,1)S(1)} %convert_element_type.130), channel_id=1, source_target_pairs={{0,1},{1,2},{2,3},{3,4},{4,5},{5,6},{6,7},{7,8},{8,9},{9,10},{10,1... | collective-permute-start | bytes 786440 | tf_op jit(solution)/shard_map/while/body/eval_jaxpr/ppermute | solution.py:24
  767.5 17.4 %collective-permute-start.1 = (bf16[128,1024]{0,1:T(8,128)(2,1)S(1)}, bf16[128,1024]{0,1:T(8,128)(2,1)}, u32[]{:S(2)}, u32[]{:S(2)}) collective-permute-start(bf16[128,1024]{0,1:T(8,128)(2,1)S(1)} %convert_element_type.130), channel_id=1, source_target_pairs={{0,1},{1,2},{2,3},{3,4},{4,5},{5,6},{6,7},{7,8},{8,9},{9,10},{10,1... | collective-permute-start | bytes 786440 | tf_op jit(solution)/shard_map/while/body/eval_jaxpr/ppermute | solution.py:24
Sparse Core Ops, SparseCore 0:
  815.8 661.2 reduce-scatter.3
